TPU v7x, 32 devices: a whole 2x2x4 slice. The times are simulated.
32 devices in a mesh: section: 4 (over y, x), dp: 8 (over z, core).
Axes of the slice: x: 2, y: 2, z: 4, core: 2. Of those that a mesh axis runs over, the one named last changes fastest.
Arguments:
- failed: int32 [8], P('dp'), may hold values from 0 to 3
- unfinished: int32 [8, 2], P('dp'), may hold values from 0 to 7, as said below
- lengths: int32 [8, 2], P('dp'), may hold values from 1 to 64
- acts: bfloat16 [4, 16, 64, 4096], P('section', 'dp'), may hold values from -100 to 100
- out_grads: bfloat16 [4, 64, 64, 512], P('section', 'dp'), may hold values from -30 to 30
- shadow_weight: bfloat16 [4, 4096, 512], P('section'), may hold values from -0.09375 to 0.09375
- shadow_gain: bfloat16 [4, 4096], P('section'), may hold values from 0.099609375 to 1.8984375
Outputs:
- in_grad: bfloat16 [4, 16, 64, 4096], P('section', 'dp')
- gain_grad: float32 [4, 4096], P('section', 'dp')
- bias_grad: float32 [4, 512], P('section', 'dp')
Inputs may be any that keep to these rules, and one draw needn't show every extreme that they name: `unfinished`: in each replica's row the 2 ids differ.
All inputs are finite; a program needn't handle non-finite values.
Results may differ from a plain program's by a relative error of at most 0.001.
Values may be sent and summed in bfloat16 or wider, within the bound.
A program may use at most 64 MiB of HBM per device.

v0:
```python
import jax
import jax.numpy as jnp
from jax import lax
from jax.sharding import PartitionSpec as P

EPSILON = 1e-06


def passed_along(value, axis, steps):
    count = lax.axis_size(axis)
    pairs = [(source, (source + steps) % count) for source in range(count)]
    return lax.ppermute(value, axis, pairs)


def pick_live(block, picked_ids, live_len):
    chosen = jnp.take(block, picked_ids, axis=0)
    position = lax.broadcasted_iota(jnp.int32, chosen.shape[:2], 1)
    live = position < live_len[:, None]
    return jnp.where(live[..., None], chosen, jnp.zeros_like(chosen))


def local_backward(rows, grads, weight, gain, replicas):
    wide = rows.astype(jnp.float32)
    inv_rms = lax.rsqrt(jnp.mean(wide * wide, axis=1, keepdims=True) + EPSILON)
    normed = wide * inv_rms
    grad_norm = lax.dot_general(
        grads, weight, (((1,), (1,)), ((), ())), preferred_element_type=jnp.float32
    )
    grad_hat = grad_norm * gain.astype(jnp.float32)[None, :]
    inner = jnp.mean(grad_hat * normed, axis=1, keepdims=True)
    result = (inv_rms * (grad_hat - normed * inner)).astype(jnp.bfloat16)
    gain_part = jnp.sum(grad_norm * normed, axis=0) / replicas
    bias_part = jnp.sum(grads.astype(jnp.float32), axis=0) / replicas
    return (result, gain_part, bias_part)


def per_device(failed, unfinished, lengths, acts, out_grads, shadow_weight, shadow_gain):
    sections = lax.axis_size("section")
    replicas = lax.axis_size("dp")
    broken = failed[0]
    helper = (broken + sections - 1) % sections
    my_section = lax.axis_index("section")
    on_helper = my_section == helper
    picked_ids = unfinished[0]
    live_len = lengths[0]
    slot_count, seq_len, channels = (acts.shape[1], acts.shape[2], acts.shape[3])
    features = out_grads.shape[3]
    total_rows = slot_count * seq_len
    outgoing = out_grads[0]
    incoming = outgoing
    for step in range(2):
        incoming = passed_along(incoming, "section", -1)
    grads = pick_live(incoming, picked_ids, live_len)
    collected, gain_part, bias_part = local_backward(
        acts[0].reshape(total_rows, channels),
        grads.reshape(total_rows, features),
        shadow_weight[0],
        shadow_gain[0],
        replicas,
    )
    collected = jnp.where(on_helper, collected, jnp.zeros_like(collected))
    gain_part = jnp.where(on_helper, gain_part, jnp.zeros_like(gain_part))
    bias_part = jnp.where(on_helper, bias_part, jnp.zeros_like(bias_part))
    gain_share, bias_share = (
        lax.psum_scatter(gain_part, "dp", scatter_dimension=0, tiled=True),
        lax.psum_scatter(bias_part, "dp", scatter_dimension=0, tiled=True),
    )
    in_grad = collected.reshape(1, slot_count, seq_len, channels)
    return (in_grad, gain_share[None, :], bias_share[None, :])


def solution(mesh):
    in_specs = (
        P("dp"),
        P("dp", None),
        P("dp", None),
        P("section", "dp", None, None),
        P("section", "dp", None, None),
        P("section", None, None),
        P("section", None),
    )
    out_specs = (P("section", "dp", None, None), P("section", "dp"), P("section", "dp"))
    return jax.shard_map(
        per_device, mesh=mesh, in_specs=in_specs, out_specs=out_specs, check_vma=False
    )
```

profile of v0, /device:TPU:0, one launch (start us, length us, event | category | flops | bytes accessed | tf_op | source)
XLA Modules:
  0.0 64.1 jit_solution(59480624349538958)
XLA Ops:
  0.6 0.0 copy-start
  0.6 3.9 %collective-permute-start = (bf16[8,64,512]{2,1,0:T(8,128)(2,1)}, bf16[8,64,512]{2,1,0:T(8,128)(2,1)S(1)}, u32[]{:S(2)}, u32[]{:S(2)}) collective-permute-start(bf16[8,64,512]{2,1,0:T(8,128)(2,1)} %bitcast.37), channel_id=1, source_target_pairs={{0,24},{8,0},{16,8},{24,16},{1,25},{9,1},{17,9},{25,17},{2,26},{10... | collective-permute-start | bytes 1572872 | tf_op jit(solution)/shard_map/ppermute | solution.py:12
  4.6 1.5 %multiply_reduce_fusion.2 = f32[2,64]{1,0:T(2,128)S(1)} fusion(bf16[1,2,64,4096]{3,2,1,0:T(8,128)(2,1)} %param.10), kind=kLoop, calls=%fused_computation.7 | loop fusion | flops 1572736 | bytes 1049088 | tf_op jit(solution)/shard_map/reduce_sum | solution.py:24
  6.8 1.2 %dynamic-slice = u32[1]{0:T(128)} dynamic-slice(u32[32]{0:T(128)} %constant.65, u32[]{:T(128)S(6)} %add.46), dynamic_slice_sizes={1} | dynamic-slice | bytes 12
  9.3 0.1 rsqrt.12
  9.4 0.7 %mul.57 = f32[1,4096]{1,0:T(1,128)S(1)} convert(bf16[1,4096]{1,0:T(2,128)(2,1)} %param.13) | non-fusion elementwise | flops 4096 | bytes 24576 | tf_op jit(solution)/shard_map/mul | solution.py:29
  10.2 0.7 %fusion.3 = s32[2]{0:T(128)S(1)} fusion(s32[1,2]{1,0:T(1,128)} %param.8), kind=kLoop, calls=%fused_computation.19 | loop fusion | flops 6 | bytes 16 | tf_op jit(solution)/shard_map/jit(_take)/jit(_where)/select_n | solution.py:16
  10.8 5.3 %collective-permute-done = bf16[8,64,512]{2,1,0:T(8,128)(2,1)S(1)} collective-permute-done((bf16[8,64,512]{2,1,0:T(8,128)(2,1)}, bf16[8,64,512]{2,1,0:T(8,128)(2,1)S(1)}, u32[]{:S(2)}, u32[]{:S(2)}) %collective-permute-start) | collective-permute-done | bytes 524320 | tf_op jit(solution)/shard_map/ppermute | solution.py:12
  16.1 3.3 %collective-permute-start.1 = (bf16[8,64,512]{2,1,0:T(8,128)(2,1)S(1)}, bf16[8,64,512]{2,1,0:T(8,128)(2,1)S(1)}, u32[]{:S(2)}, u32[]{:S(2)}) collective-permute-start(bf16[8,64,512]{2,1,0:T(8,128)(2,1)S(1)} %collective-permute-done), channel_id=1, source_target_pairs={{0,24},{8,0},{16,8},{24,16},{1,25},{9,1},{17,9},{25,17},{2,26},{10... | collective-permute-start | bytes 1572872 | tf_op jit(solution)/shard_map/ppermute | solution.py:12
  19.4 0.7 %compare_and_fusion = pred[2]{0:T(512)(128)(4,1)S(1)} fusion(s32[1,2]{1,0:T(1,128)} %param.8), kind=kLoop, calls=%fused_computation.16 | loop fusion | flops 12 | bytes 10 | tf_op jit(solution)/shard_map/jit(_take)/and | solution.py:16
  20.0 0.7 %iota_compare_fusion = pred[2,64]{1,0:T(4,128)(4,1)S(1)} fusion(s32[2]{0:T(128)} %bitcast.38), kind=kLoop, calls=%fused_computation.17 | loop fusion | flops 128 | bytes 136 | tf_op jit(solution)/shard_map/lt | solution.py:18
  20.8 8.9 %collective-permute-done.1 = bf16[8,64,512]{2,1,0:T(8,128)(2,1)S(1)} collective-permute-done((bf16[8,64,512]{2,1,0:T(8,128)(2,1)S(1)}, bf16[8,64,512]{2,1,0:T(8,128)(2,1)S(1)}, u32[]{:S(2)}, u32[]{:S(2)}) %collective-permute-start.1) | collective-permute-done | bytes 524320 | tf_op jit(solution)/shard_map/ppermute | solution.py:12
  29.7 0.6 gather_fusion
  30.2 0.1 convert_reduce_fusion
  30.4 0.0 copy-done
  30.4 3.8 %multiply_reduce_fusion = (f32[4096]{0:T(1024)S(1)}, f32[128]{0:T(128)S(1)}, f32[128,4096]{1,0:T(8,128)S(1)}) fusion(bf16[1,2,64,4096]{3,2,1,0:T(8,128)(2,1)S(1)} %copy-done, f32[128]{0:T(128)S(1)} %rsqrt.12, f32[4096]{0:T(1024)S(1)} %bitcast.34, bf16[128,512]{1,0:T(8,128)(2,1)S(1)} %bitcast.33, bf16[1,4096,512]{2,1,0:T(8,128)(2,1)} %param.12), kind=kOutput, calls=%fused_computation.4 | convolution fusion | flops 540536704 | bytes 7504896 | tf_op jit(solution)/shard_map/dot_general | solution.py:26
  34.2 27.1 %all-reduce.2 = (f32[4096]{0:T(1024)S(1)}, f32[512]{0:T(512)S(1)}) all-reduce(f32[4096]{0:T(1024)S(1)} %multiply_select_fusion, f32[512]{0:T(512)S(1)} %multiply_select_fusion.1), channel_id=2, replica_groups=mesh['section'=4,'dp'=8] {'dp'}, use_global_device_ids=true, to_apply=%region_3.4.clone | all-reduce | flops 4608 | bytes 36864
  61.3 0.7 %dynamic-slice.1 = f32[512]{0:T(512)} dynamic-slice(f32[4096]{0:T(1024)S(1)} %get-tuple-element.5, u32[]{:T(128)S(6)} %multiply.16), dynamic_slice_sizes={512} | dynamic-slice | bytes 4100
  61.9 0.6 dynamic-slice_bitcast_fusion
  62.5 1.6 %fusion.2 = bf16[128,4096]{1,0:T(8,128)(2,1)} fusion(bf16[1,2,64,4096]{3,2,1,0:T(8,128)(2,1)S(1)} %copy-done, f32[128,4096]{1,0:T(8,128)S(1)} %get-tuple-element.9, f32[128]{0:T(128)S(1)} %broadcast_multiply_fusion, f32[4096]{0:T(1024)S(1)} %bitcast.35, f32[128]{0:T(128)S(1)} %rsqrt.12, pred[]{:T(512)S(6)} %eq.5), kind=kLoop, calls=%fused_computation.8 | loop fusion | flops 4194304 | bytes 4211713 | tf_op jit(solution)/shard_map/jit(_where)/select_n | solution.py:61
  (5 shorter events, 0.0 us)
Async XLA Ops:
  0.6 29.7 %copy-start = (bf16[1,2,64,4096]{3,2,1,0:T(8,128)(2,1)S(1)}, bf16[1,2,64,4096]{3,2,1,0:T(8,128)(2,1)}, u32[]{:S(2)}) copy-start(bf16[1,2,64,4096]{3,2,1,0:T(8,128)(2,1)} %param.10) | copy-start | bytes 3145732
  0.6 15.4 %collective-permute-start = (bf16[8,64,512]{2,1,0:T(8,128)(2,1)}, bf16[8,64,512]{2,1,0:T(8,128)(2,1)S(1)}, u32[]{:S(2)}, u32[]{:S(2)}) collective-permute-start(bf16[8,64,512]{2,1,0:T(8,128)(2,1)} %bitcast.37), channel_id=1, source_target_pairs={{0,24},{8,0},{16,8},{24,16},{1,25},{9,1},{17,9},{25,17},{2,26},{10... | collective-permute-start | bytes 1572872 | tf_op jit(solution)/shard_map/ppermute | solution.py:12
  16.1 13.6 %collective-permute-start.1 = (bf16[8,64,512]{2,1,0:T(8,128)(2,1)S(1)}, bf16[8,64,512]{2,1,0:T(8,128)(2,1)S(1)}, u32[]{:S(2)}, u32[]{:S(2)}) collective-permute-start(bf16[8,64,512]{2,1,0:T(8,128)(2,1)S(1)} %collective-permute-done), channel_id=1, source_target_pairs={{0,24},{8,0},{16,8},{24,16},{1,25},{9,1},{17,9},{25,17},{2,26},{10... | collective-permute-start | bytes 1572872 | tf_op jit(solution)/shard_map/ppermute | solution.py:12
where the time goes:
time: 64.4 us; the launch traced here: 64.1 us
  blocking collectives  27.1 us (42%)
  waiting for transfers between devices  14.2 us (22%)
  starting transfers between devices  7.22 us (11%)
  other arithmetic  6.01 us (9%)
  matrix products  3.79 us (6%)
  local copies, waits for them, and re-layouts  3.11 us (5%)
  between operations  2.68 us (4%)
    unnamed x1, blocking collectives  27.1 us
    ppermute x2, waiting for transfers between devices, passed_along(): return lax.ppermute(value, axis, pairs)  14.2 us
    ppermute x2, starting transfers between devices, passed_along(): return lax.ppermute(value, axis, pairs)  7.22 us
    dot_general x1, matrix products, local_backward(): lax.dot_general(grads, weight, (((1,), (1,)), ((), ())), preferred_elemen...  3.79 us
    unnamed x4, local copies, waits for them, and re-layouts  1.9 us
    select_n x1, other arithmetic, per_device(): collected = jnp.where(on_helper, collected, jnp.zeros_like(collected))  1.56 us
    reduce_sum x1, other arithmetic, local_backward(): inv_rms = lax.rsqrt(jnp.mean(wide * wide, axis=1, keepdims=True) + EPSILON)  1.52 us
  transfers between devices with their start and end apart: 2, of which 2 were waited for; matrix products, arithmetic and copies ran while one was open for 9% of the time, Pallas kernels for 0%

commit v1 on v0

v1 whole, which is shorter than its diff:
```python
import functools

import jax
import jax.numpy as jnp
from jax import lax
from jax.experimental import pallas as pl
from jax.experimental.pallas import tpu as pltpu
from jax.sharding import PartitionSpec as P

EPSILON = 1e-06
MESH = pl.DeviceIdType.MESH
LANES = 128
HALVES = 2
TILE = 256
ROWS = 16


def recover_kernel(
    sections,
    replicas,
    failed,
    unfinished,
    lengths,
    gain_ref,
    acts_hbm,
    out_grads_hbm,
    weight_hbm,
    dx_ref,
    share_ref,
    acts,
    out_grads,
    weight,
    send,
    recv,
    normed,
    inv_rms,
    grad_norm,
    parts_out,
    parts_in,
    load_sem,
    send_sem,
    recv_sem,
    part_send_sem,
    part_recv_sem,
):
    section = lax.axis_index("section")
    replica = lax.axis_index("dp")
    slots, seq = unfinished.shape[1], out_grads.shape[1]
    features, half = out_grads.shape[2], out_grads.shape[2] // HALVES
    rows, channels = acts.shape
    gain_share, bias_share = channels // replicas, features // replicas
    gain_chunk = max(gain_share, LANES)
    group = gain_chunk // gain_share
    chunks = channels // gain_chunk
    gain_rows = gain_chunk // LANES

    loads = [
        pltpu.make_async_copy(source, target, load_sem.at[i])
        for i, (source, target) in enumerate(
            ((out_grads_hbm, out_grads), (acts_hbm, acts), (weight_hbm, weight))
        )
    ]
    for load in loads:
        load.start()

    target = lax.rem(section + sections - 2, sections)
    origin = lax.rem(section + 2, sections)
    barrier = pltpu.get_barrier_semaphore()
    greeted = 1
    pl.semaphore_signal(barrier, inc=1, device_id={"section": origin}, device_id_type=MESH)
    if (sections - 2) % sections != 2 % sections:
        greeted = 2
        pl.semaphore_signal(barrier, inc=1, device_id={"section": target}, device_id_type=MESH)
    for step in range(1, replicas):
        peer = lax.rem(replica + step, replicas)
        pl.semaphore_signal(barrier, inc=1, device_id={"dp": peer}, device_id_type=MESH)

    is_source = lax.rem(failed[0] + 1, sections) == section
    loads[0].wait()
    for slot in range(slots):
        picked = out_grads[unfinished[0, slot]].astype(jnp.float32)
        limit = jnp.where(is_source, lengths[0, slot], 0)
        position = lax.broadcasted_iota(jnp.int32, picked.shape, 0)
        picked = jnp.where(position < limit, picked, 0.0).astype(jnp.bfloat16)
        for part in range(HALVES):
            send[part, slot * seq : (slot + 1) * seq, :] = picked[:, part * half : (part + 1) * half]

    pl.semaphore_wait(barrier, greeted + replicas - 1)
    copies = []
    for part in range(HALVES):
        copy = pltpu.make_async_remote_copy(
            src_ref=send.at[part],
            dst_ref=recv.at[part],
            send_sem=send_sem.at[part],
            recv_sem=recv_sem.at[part],
            device_id={"section": target},
            device_id_type=MESH,
        )
        copy.start()
        copies.append(copy)

    loads[1].wait()
    for block in range(rows // ROWS):
        at = slice(block * ROWS, (block + 1) * ROWS)
        wide = acts[at, :].astype(jnp.float32)
        scale = lax.rsqrt(jnp.mean(wide * wide, axis=1, keepdims=True) + EPSILON)
        inv_rms[at, :] = jnp.broadcast_to(scale, (ROWS, LANES))
        normed[at, :] = wide * scale

    loads[2].wait()
    copies[0].wait_recv()
    for tile in range(channels // TILE):
        at = slice(tile * TILE, (tile + 1) * TILE)
        grad_norm[:, at] = lax.dot_general(
            recv[0], weight[at, :half], (((1,), (1,)), ((), ())), preferred_element_type=jnp.float32
        )

    copies[1].wait_recv()
    for part in range(HALVES):
        bias = jnp.sum(recv[part].astype(jnp.float32), axis=0, keepdims=True) / replicas
        for peer in range(replicas):
            lane = (peer * bias_share // LANES) * LANES
            if part * half <= lane < (part + 1) * half:
                lane -= part * half
                parts_out[peer, gain_rows : gain_rows + 1, :] = bias[:, lane : lane + LANES]

    inner = jnp.zeros((rows, LANES), jnp.float32)
    part_copies = []
    width = min(TILE, gain_chunk)
    first = replica // group
    for step in range(1, chunks + 1):
        chunk = lax.rem(first + step, chunks)
        for piece in range(gain_chunk // width):
            at = pl.ds(pl.multiple_of(chunk * gain_chunk + piece * width, width), width)
            value = grad_norm[:, at] + lax.dot_general(
                recv[1], weight[at, half:], (((1,), (1,)), ((), ())), preferred_element_type=jnp.float32
            )
            grad_norm[:, at] = value
            product = value * normed[:, at]
            column = jnp.sum(product, axis=0, keepdims=True) / replicas
            for g in range(group):
                for row in range(width // LANES):
                    place = piece * (width // LANES) + row
                    parts_out[chunk * group + g, place : place + 1, :] = column[:, row * LANES : (row + 1) * LANES]
            product = product * gain_ref[:, at].astype(jnp.float32)
            for row in range(width // LANES):
                inner = inner + product[:, row * LANES : (row + 1) * LANES]
        for g in range(group):
            if group == 1 and step == chunks:
                continue
            peer = chunk * group + g
            copy = pltpu.make_async_remote_copy(
                src_ref=parts_out.at[peer],
                dst_ref=parts_in.at[replica],
                send_sem=part_send_sem.at[peer],
                recv_sem=part_recv_sem.at[replica],
                device_id={"dp": peer},
                device_id_type=MESH,
            )
            if group == 1:
                copy.start()
            else:
                pl.when(peer != replica)(copy.start)
    parts_in[replica] = parts_out[replica]

    inner = jnp.sum(inner, axis=1, keepdims=True) / channels
    gain = gain_ref[...].astype(jnp.float32)
    for block in range(rows // ROWS):
        at = slice(block * ROWS, (block + 1) * ROWS)
        result = inv_rms[at, :1] * (grad_norm[at, :] * gain - normed[at, :] * inner[at])
        dx_ref[at, :] = result.astype(jnp.bfloat16)

    for step in range(1, replicas):
        peer = lax.rem(replica + step, replicas)
        copy = pltpu.make_async_remote_copy(
            src_ref=parts_out.at[peer],
            dst_ref=parts_in.at[peer],
            send_sem=part_send_sem.at[peer],
            recv_sem=part_recv_sem.at[peer],
            device_id={"dp": peer},
            device_id_type=MESH,
        )
        copy.wait_recv()
        copy.wait_send()
    share_ref[...] = jnp.sum(parts_in[...], axis=0)
    for copy in copies:
        copy.wait_send()


def own_lanes(value, replica, share):
    if share >= LANES:
        return value
    options = LANES // share
    own = value[:, :share]
    for option in range(1, options):
        other = value[:, option * share : (option + 1) * share]
        own = jnp.where(lax.rem(replica, options) == option, other, own)
    return own


def write_kernel(dx, share, in_grad, gain_grad, bias_grad, sem):
    copy = pltpu.make_async_copy(dx, in_grad, sem)
    copy.start()
    replica = lax.axis_index("dp")
    gain_share, bias_share = gain_grad.shape[1], bias_grad.shape[1]
    gain_rows = max(gain_share, LANES) // LANES
    if gain_rows == 1:
        gain_grad[...] = own_lanes(share[:1, :], replica, gain_share)
    else:
        for row in range(gain_rows):
            gain_grad[:, row * LANES : (row + 1) * LANES] = share[row : row + 1, :]
    bias_grad[...] = own_lanes(share[gain_rows : gain_rows + 1, :], replica, bias_share)
    copy.wait()


def per_device(failed, unfinished, lengths, acts, out_grads, shadow_weight, shadow_gain):
    sections = lax.axis_size("section")
    replicas = lax.axis_size("dp")
    slots, seq, channels = acts.shape[1:]
    features = out_grads.shape[3]
    rows = slots * seq
    gain_rows = max(channels // replicas, LANES) // LANES
    packed = -(-(gain_rows + 1) // 8) * 8
    f32, bf16 = jnp.float32, jnp.bfloat16
    smem = pl.BlockSpec(memory_space=pltpu.SMEM)
    vmem = pl.BlockSpec(memory_space=pltpu.VMEM)
    hbm = pl.BlockSpec(memory_space=pltpu.HBM)
    dx, share = pl.pallas_call(
        functools.partial(recover_kernel, sections, replicas),
        out_shape=(
            pltpu.VMEM((rows, channels), bf16),
            pltpu.VMEM((packed, LANES), f32),
        ),
        in_specs=[smem, smem, smem, vmem, hbm, hbm, hbm],
        out_specs=(vmem, vmem),
        scratch_shapes=[
            pltpu.VMEM((rows, channels), bf16),
            pltpu.VMEM(out_grads.shape[1:], bf16),
            pltpu.VMEM((channels, features), bf16),
            pltpu.VMEM((HALVES, rows, features // HALVES), bf16),
            pltpu.VMEM((HALVES, rows, features // HALVES), bf16),
            pltpu.VMEM((rows, channels), f32),
            pltpu.VMEM((rows, LANES), f32),
            pltpu.VMEM((rows, channels), f32),
            pltpu.VMEM((replicas, packed, LANES), f32),
            pltpu.VMEM((replicas, packed, LANES), f32),
            pltpu.SemaphoreType.DMA((3,)),
            pltpu.SemaphoreType.DMA((HALVES,)),
            pltpu.SemaphoreType.DMA((HALVES,)),
            pltpu.SemaphoreType.DMA((replicas,)),
            pltpu.SemaphoreType.DMA((replicas,)),
        ],
        compiler_params=pltpu.CompilerParams(
            collective_id=0, has_side_effects=True, vmem_limit_bytes=28 * 2**20
        ),
        cost_estimate=pl.CostEstimate(
            flops=2 * rows * features * channels,
            bytes_accessed=2 * (channels * features + 2 * rows * channels),
            transcendentals=rows,
        ),
        name="recover",
    )(
        failed,
        unfinished,
        lengths,
        shadow_gain,
        *(
            pltpu.with_memory_space_constraint(operand, pltpu.HBM)
            for operand in (acts.reshape(rows, channels), out_grads[0], shadow_weight[0])
        ),
    )
    in_grad, gain_grad, bias_grad = pl.pallas_call(
        write_kernel,
        out_shape=(
            jax.ShapeDtypeStruct((rows, channels), bf16),
            jax.ShapeDtypeStruct((1, channels // replicas), f32),
            jax.ShapeDtypeStruct((1, features // replicas), f32),
        ),
        in_specs=[vmem, vmem],
        out_specs=(hbm, vmem, vmem),
        scratch_shapes=[pltpu.SemaphoreType.DMA],
        compiler_params=pltpu.CompilerParams(vmem_limit_bytes=8 * 2**20),
        cost_estimate=pl.CostEstimate(
            flops=0, bytes_accessed=4 * rows * channels, transcendentals=0
        ),
        name="write",
    )(dx, share)
    return in_grad.reshape(1, slots, seq, channels), gain_grad, bias_grad


def solution(mesh):
    in_specs = (
        P("dp"),
        P("dp", None),
        P("dp", None),
        P("section", "dp", None, None),
        P("section", "dp", None, None),
        P("section", None, None),
        P("section", None),
    )
    out_specs = (P("section", "dp", None, None), P("section", "dp"), P("section", "dp"))
    return jax.shard_map(
        per_device, mesh=mesh, in_specs=in_specs, out_specs=out_specs, check_vma=False
    )
```

time: 64.4 us -> 20.1 us (0.31)
  blocking collectives: 27.1 us -> 0 us
  Pallas kernels: 0 us -> 16.5 us
  waiting for transfers between devices: 14.2 us -> 0 us
  starting transfers between devices: 7.22 us -> 0 us
  other arithmetic: 6.01 us -> 0 us
  matrix products: 3.79 us -> 0 us
  between operations: 2.68 us -> 1.3 us
  local copies, waits for them, and re-layouts: 3.11 us -> 2.02 us
    unnamed x1 -> x0, blocking collectives: 27.1 us -> none
    pallas_call x0 -> x2, Pallas kernels: none -> 16.5 us  [the longest x1 15 us: per_device(): pl.pallas_call(functools.partial(recover_kernel, sections, replicas), out...]
    ppermute x2 -> x0, waiting for transfers between devices: 14.2 us -> none  [passed_along(): return lax.ppermute(value, axis, pairs)]
    ppermute x2 -> x0, starting transfers between devices: 7.22 us -> none  [passed_along(): return lax.ppermute(value, axis, pairs)]
    dot_general x1 -> x0, matrix products: 3.79 us -> none  [local_backward(): lax.dot_general(grads, weight, (((1,), (1,)), ((), ())), preferred_elemen...]
    select_n x4 -> x0, other arithmetic: 2.23 us -> none  [the longest x1 1.56 us: per_device(): collected = jnp.where(on_helper, collected, jnp.zeros_like(collected))]
    reduce_sum x2 -> x0, other arithmetic: 1.64 us -> none  [the longest x1 1.52 us: local_backward(): inv_rms = lax.rsqrt(jnp.mean(wide * wide, axis=1, keepdims=True) + EPSILON)]
    mul x1 -> x0, other arithmetic: 0.74 us -> none  [local_backward(): grad_hat = grad_norm * gain.astype(jnp.float32)[None, :]]
  transfers between devices with their start and end apart: 2 -> 0, of which waited for: 2 -> 0; matrix products, arithmetic and copies ran while one was open for 9% -> 0% of each run, Pallas kernels for 0% -> 0%
where the time goes in v1:
time: 20.1 us; the launch traced here: 19.9 us
  Pallas kernels  16.5 us (82%)
  local copies, waits for them, and re-layouts  2.02 us (10%)
  between operations  1.3 us (6%)
    pallas_call x1, Pallas kernels, per_device(): pl.pallas_call(functools.partial(recover_kernel, sections, replicas), out...  15 us
    unnamed x6, local copies, waits for them, and re-layouts  2.02 us
    pallas_call x1, Pallas kernels, per_device(): pl.pallas_call(write_kernel, out_shape=(jax.ShapeDtypeStruct((rows, chann...  1.56 us

profile of v1, /device:TPU:0, one launch (start us, length us, event | category | flops | bytes accessed | tf_op | source)
XLA Modules:
  0.0 19.9 jit_solution(15721346930864638825)
XLA Ops:
  1.3 0.0 copy-start
  1.3 0.7 %copy-done = bf16[1,4096]{1,0:T(2,128)(2,1)S(1)} copy-done((bf16[1,4096]{1,0:T(2,128)(2,1)S(1)}, bf16[1,4096]{1,0:T(2,128)(2,1)}, u32[]{:S(2)}) %copy-start) | copy-done | bytes 8216
  2.0 0.0 copy-start.1
  2.0 0.7 %copy-done.1 = s32[1,2]{1,0:T(1,128)S(1)} copy-done((s32[1,2]{1,0:T(1,128)S(1)}, s32[1,2]{1,0:T(1,128)}, u32[]{:S(2)}) %copy-start.1) | copy-done | bytes 32
  2.7 0.0 copy-start.2
  2.7 0.7 %copy-done.2 = s32[1,2]{1,0:T(1,128)S(1)} copy-done((s32[1,2]{1,0:T(1,128)S(1)}, s32[1,2]{1,0:T(1,128)}, u32[]{:S(2)}) %copy-start.2) | copy-done | bytes 32
  3.3 15.0 %recover.1 = (bf16[128,4096]{1,0:T(8,128)(2,1)S(1)}, f32[8,128]{1,0:T(8,128)S(1)}) custom-call(s32[1]{0:T(128)S(6)} %copy.10.failed, s32[1,2]{1,0:T(1,128)S(1)} %copy-done.1, s32[1,2]{1,0:T(1,128)S(1)} %copy-done.2, bf16[1,4096]{1,0:T(2,128)(2,1)S(1)} %copy-done, bf16[128,4096]{1,0:T(8,128)(2,1)} %bitcast.5, bf16[8,64,512]{2,1,0:T(8,128)(2,1)} %bitcast.6, ...), custom_call_target="tpu_custom_call" | custom-call | flops 536870912 | bytes 6291456 | tf_op jit(solution)/shard_map/recover/pallas_call | solution.py:228
  18.3 1.6 %write.1 = (bf16[128,4096]{1,0:T(8,128)(2,1)}, f32[1,512]{1,0:T(1,128)}, f32[1,64]{1,0:T(1,128)}) custom-call(bf16[128,4096]{1,0:T(8,128)(2,1)S(1)} %get-tuple-element.8.dx, f32[8,128]{1,0:T(8,128)S(1)} %get-tuple-element.9.share), custom_call_target="tpu_custom_call" | custom-call | bytes 2097152 | tf_op jit(solution)/shard_map/write/pallas_call | solution.py:272
Async XLA Ops:
  1.3 0.7 %copy-start = (bf16[1,4096]{1,0:T(2,128)(2,1)S(1)}, bf16[1,4096]{1,0:T(2,128)(2,1)}, u32[]{:S(2)}) copy-start(bf16[1,4096]{1,0:T(2,128)(2,1)} %gain_ref.1) | copy-start | bytes 24580
  2.0 0.7 %copy-start.1 = (s32[1,2]{1,0:T(1,128)S(1)}, s32[1,2]{1,0:T(1,128)}, u32[]{:S(2)}) copy-start(s32[1,2]{1,0:T(1,128)} %unfinished.1) | copy-start | bytes 28
  2.7 0.7 %copy-start.2 = (s32[1,2]{1,0:T(1,128)S(1)}, s32[1,2]{1,0:T(1,128)}, u32[]{:S(2)}) copy-start(s32[1,2]{1,0:T(1,128)} %lengths.1) | copy-start | bytes 28

commit v2 on v1

--- a/solution.py
+++ b/solution.py
@@ -13,20 +13,24 @@
 HALVES = 2
 TILE = 256
 ROWS = 16
+PIECES = 4
 
 
 def recover_kernel(
     sections,
     replicas,
     failed,
-    unfinished,
-    lengths,
-    gain_ref,
+    unfinished_hbm,
+    lengths_hbm,
+    gain_hbm,
     acts_hbm,
     out_grads_hbm,
     weight_hbm,
     dx_ref,
     share_ref,
+    unfinished,
+    lengths,
+    gain_ref,
     acts,
     out_grads,
     weight,
@@ -57,12 +61,16 @@
     loads = [
         pltpu.make_async_copy(source, target, load_sem.at[i])
         for i, (source, target) in enumerate(
-            ((out_grads_hbm, out_grads), (acts_hbm, acts), (weight_hbm, weight))
+            (
+                (unfinished_hbm, unfinished),
+                (lengths_hbm, lengths),
+                (out_grads_hbm, out_grads),
+                (acts_hbm, acts),
+                (gain_hbm, gain_ref),
+                (weight_hbm, weight),
+            )
         )
     ]
-    for load in loads:
-        load.start()
-
     target = lax.rem(section + sections - 2, sections)
     origin = lax.rem(section + 2, sections)
     barrier = pltpu.get_barrier_semaphore()
@@ -75,8 +83,13 @@
         peer = lax.rem(replica + step, replicas)
         pl.semaphore_signal(barrier, inc=1, device_id={"dp": peer}, device_id_type=MESH)
 
+    for load in loads[:4]:
+        load.start()
+    for load in loads[:3]:
+        load.wait()
+    for load in loads[4:]:
+        load.start()
     is_source = lax.rem(failed[0] + 1, sections) == section
-    loads[0].wait()
     for slot in range(slots):
         picked = out_grads[unfinished[0, slot]].astype(jnp.float32)
         limit = jnp.where(is_source, lengths[0, slot], 0)
@@ -99,7 +112,7 @@
         copy.start()
         copies.append(copy)
 
-    loads[1].wait()
+    loads[3].wait()
     for block in range(rows // ROWS):
         at = slice(block * ROWS, (block + 1) * ROWS)
         wide = acts[at, :].astype(jnp.float32)
@@ -107,7 +120,8 @@
         inv_rms[at, :] = jnp.broadcast_to(scale, (ROWS, LANES))
         normed[at, :] = wide * scale
 
-    loads[2].wait()
+    loads[4].wait()
+    loads[5].wait()
     copies[0].wait_recv()
     for tile in range(channels // TILE):
         at = slice(tile * TILE, (tile + 1) * TILE)
@@ -198,19 +212,27 @@
     return own
 
 
-def write_kernel(dx, share, in_grad, gain_grad, bias_grad, sem):
-    copy = pltpu.make_async_copy(dx, in_grad, sem)
-    copy.start()
+def write_kernel(dx, share, in_grad, gain_grad, bias_grad, gain, bias, sem):
+    rows = dx.shape[0]
+    copies = []
+    for i in range(PIECES):
+        at = pl.ds(i * (rows // PIECES), rows // PIECES)
+        copies.append(pltpu.make_async_copy(dx.at[at], in_grad.at[at], sem.at[i]))
+        copies[-1].start()
     replica = lax.axis_index("dp")
-    gain_share, bias_share = gain_grad.shape[1], bias_grad.shape[1]
+    gain_share, bias_share = gain.shape[1], bias.shape[1]
     gain_rows = max(gain_share, LANES) // LANES
     if gain_rows == 1:
-        gain_grad[...] = own_lanes(share[:1, :], replica, gain_share)
+        gain[...] = own_lanes(share[:1, :], replica, gain_share)
     else:
         for row in range(gain_rows):
-            gain_grad[:, row * LANES : (row + 1) * LANES] = share[row : row + 1, :]
-    bias_grad[...] = own_lanes(share[gain_rows : gain_rows + 1, :], replica, bias_share)
-    copy.wait()
+            gain[:, row * LANES : (row + 1) * LANES] = share[row : row + 1, :]
+    bias[...] = own_lanes(share[gain_rows : gain_rows + 1, :], replica, bias_share)
+    for i, (source, target) in enumerate(((gain, gain_grad), (bias, bias_grad))):
+        copies.append(pltpu.make_async_copy(source, target, sem.at[PIECES + i]))
+        copies[-1].start()
+    for copy in copies:
+        copy.wait()
 
 
 def per_device(failed, unfinished, lengths, acts, out_grads, shadow_weight, shadow_gain):
@@ -222,7 +244,6 @@
     gain_rows = max(channels // replicas, LANES) // LANES
     packed = -(-(gain_rows + 1) // 8) * 8
     f32, bf16 = jnp.float32, jnp.bfloat16
-    smem = pl.BlockSpec(memory_space=pltpu.SMEM)
     vmem = pl.BlockSpec(memory_space=pltpu.VMEM)
     hbm = pl.BlockSpec(memory_space=pltpu.HBM)
     dx, share = pl.pallas_call(
@@ -231,9 +252,12 @@
             pltpu.VMEM((rows, channels), bf16),
             pltpu.VMEM((packed, LANES), f32),
         ),
-        in_specs=[smem, smem, smem, vmem, hbm, hbm, hbm],
+        in_specs=[pl.BlockSpec(memory_space=pltpu.SMEM)] + [hbm] * 6,
         out_specs=(vmem, vmem),
         scratch_shapes=[
+            pltpu.SMEM(unfinished.shape, jnp.int32),
+            pltpu.SMEM(lengths.shape, jnp.int32),
+            pltpu.VMEM(shadow_gain.shape, bf16),
             pltpu.VMEM((rows, channels), bf16),
             pltpu.VMEM(out_grads.shape[1:], bf16),
             pltpu.VMEM((channels, features), bf16),
@@ -244,7 +268,7 @@
             pltpu.VMEM((rows, channels), f32),
             pltpu.VMEM((replicas, packed, LANES), f32),
             pltpu.VMEM((replicas, packed, LANES), f32),
-            pltpu.SemaphoreType.DMA((3,)),
+            pltpu.SemaphoreType.DMA((6,)),
             pltpu.SemaphoreType.DMA((HALVES,)),
             pltpu.SemaphoreType.DMA((HALVES,)),
             pltpu.SemaphoreType.DMA((replicas,)),
@@ -261,12 +285,16 @@
         name="recover",
     )(
         failed,
-        unfinished,
-        lengths,
-        shadow_gain,
         *(
             pltpu.with_memory_space_constraint(operand, pltpu.HBM)
-            for operand in (acts.reshape(rows, channels), out_grads[0], shadow_weight[0])
+            for operand in (
+                unfinished,
+                lengths,
+                shadow_gain,
+                acts.reshape(rows, channels),
+                out_grads[0],
+                shadow_weight[0],
+            )
         ),
     )
     in_grad, gain_grad, bias_grad = pl.pallas_call(
@@ -277,8 +305,12 @@
             jax.ShapeDtypeStruct((1, features // replicas), f32),
         ),
         in_specs=[vmem, vmem],
-        out_specs=(hbm, vmem, vmem),
-        scratch_shapes=[pltpu.SemaphoreType.DMA],
+        out_specs=(hbm, hbm, hbm),
+        scratch_shapes=[
+            pltpu.VMEM((1, channels // replicas), f32),
+            pltpu.VMEM((1, features // replicas), f32),
+            pltpu.SemaphoreType.DMA((PIECES + 2,)),
+        ],
         compiler_params=pltpu.CompilerParams(vmem_limit_bytes=8 * 2**20),
         cost_estimate=pl.CostEstimate(
             flops=0, bytes_accessed=4 * rows * channels, transcendentals=0

time: 20.1 us -> 16.9 us (0.84)
  local copies, waits for them, and re-layouts: 2.02 us -> 0 us
  Pallas kernels: 16.5 us -> 15.5 us
    unnamed x6 -> x0, local copies, waits for them, and re-layouts: 2.02 us -> none
    pallas_call x1, Pallas kernels: 1.56 us -> 1.02 us  [per_device(): pl.pallas_call(write_kernel, out_shape=(jax.ShapeDtypeStruct((rows, chann...]
    pallas_call x1, Pallas kernels: 15 us -> 14.5 us  [per_device(): pl.pallas_call(functools.partial(recover_kernel, sections, replicas), out...]
where the time goes in v2:
time: 16.9 us; the launch traced here: 16.8 us
  Pallas kernels  15.5 us (92%)
  between operations  1.29 us (8%)
    pallas_call x1, Pallas kernels, per_device(): pl.pallas_call(functools.partial(recover_kernel, sections, replicas), out...  14.5 us
    pallas_call x1, Pallas kernels, per_device(): pl.pallas_call(write_kernel, out_shape=(jax.ShapeDtypeStruct((rows, chann...  1.02 us

profile of v2, /device:TPU:0, one launch (start us, length us, event | category | flops | bytes accessed | tf_op | source)
XLA Modules:
  0.0 16.8 jit_solution(9150723659562393810)
XLA Ops:
  1.3 14.5 %recover.1 = (bf16[128,4096]{1,0:T(8,128)(2,1)S(1)}, f32[8,128]{1,0:T(8,128)S(1)}) custom-call(s32[1]{0:T(128)S(6)} %copy.10.failed, s32[1,2]{1,0:T(1,128)} %unfinished_hbm.1, s32[1,2]{1,0:T(1,128)} %lengths_hbm.1, bf16[1,4096]{1,0:T(2,128)(2,1)} %gain_hbm.1, bf16[128,4096]{1,0:T(8,128)(2,1)} %bitcast.5, bf16[8,64,512]{2,1,0:T(8,128)(2,1)} %bitcast.6, ...), custom_call_target="tpu_custom_call" | custom-call | flops 536870912 | bytes 6291456 | tf_op jit(solution)/shard_map/recover/pallas_call | solution.py:249
  15.8 1.0 %write.1 = (bf16[128,4096]{1,0:T(8,128)(2,1)}, f32[1,512]{1,0:T(1,128)}, f32[1,64]{1,0:T(1,128)}) custom-call(bf16[128,4096]{1,0:T(8,128)(2,1)S(1)} %get-tuple-element.8.dx, f32[8,128]{1,0:T(8,128)S(1)} %get-tuple-element.9.share), custom_call_target="tpu_custom_call" | custom-call | bytes 2097152 | tf_op jit(solution)/shard_map/write/pallas_call | solution.py:300

commit v3 on v2

--- a/solution.py
+++ b/solution.py
@@ -58,19 +58,29 @@
     chunks = channels // gain_chunk
     gain_rows = gain_chunk // LANES
 
-    loads = [
-        pltpu.make_async_copy(source, target, load_sem.at[i])
-        for i, (source, target) in enumerate(
-            (
-                (unfinished_hbm, unfinished),
-                (lengths_hbm, lengths),
-                (out_grads_hbm, out_grads),
-                (acts_hbm, acts),
-                (gain_hbm, gain_ref),
-                (weight_hbm, weight),
+    def load(source, target, pieces, start):
+        size = source.shape[0] // pieces
+        return [
+            pltpu.make_async_copy(
+                source.at[pl.ds(i * size, size)], target.at[pl.ds(i * size, size)], load_sem.at[start + i]
             )
-        )
-    ]
+            for i in range(pieces)
+        ]
+
+    small = load(unfinished_hbm, unfinished, 1, 0) + load(lengths_hbm, lengths, 1, 1)
+    load_gain = load(gain_hbm, gain_ref, 1, 2)
+    load_grads = load(out_grads_hbm, out_grads, PIECES, 3)
+    load_acts = load(acts_hbm, acts, PIECES, 3 + PIECES)
+    load_weight = load(weight_hbm, weight, PIECES, 3 + 2 * PIECES)
+
+    def add_bias(part):
+        bias = jnp.sum(recv[part].astype(jnp.float32), axis=0, keepdims=True) / replicas
+        for peer in range(replicas):
+            lane = (peer * bias_share // LANES) * LANES
+            if part * half <= lane < (part + 1) * half:
+                lane -= part * half
+                parts_out[peer, gain_rows : gain_rows + 1, :] = bias[:, lane : lane + LANES]
+
     target = lax.rem(section + sections - 2, sections)
     origin = lax.rem(section + 2, sections)
     barrier = pltpu.get_barrier_semaphore()
@@ -83,12 +93,12 @@
         peer = lax.rem(replica + step, replicas)
         pl.semaphore_signal(barrier, inc=1, device_id={"dp": peer}, device_id_type=MESH)
 
-    for load in loads[:4]:
-        load.start()
-    for load in loads[:3]:
-        load.wait()
-    for load in loads[4:]:
-        load.start()
+    for copy in small + load_grads:
+        copy.start()
+    for copy in small + load_grads:
+        copy.wait()
+    for copy in load_acts + load_weight + load_gain:
+        copy.start()
     is_source = lax.rem(failed[0] + 1, sections) == section
     for slot in range(slots):
         picked = out_grads[unfinished[0, slot]].astype(jnp.float32)
@@ -112,7 +122,8 @@
         copy.start()
         copies.append(copy)
 
-    loads[3].wait()
+    for copy in load_acts:
+        copy.wait()
     for block in range(rows // ROWS):
         at = slice(block * ROWS, (block + 1) * ROWS)
         wide = acts[at, :].astype(jnp.float32)
@@ -120,8 +131,8 @@
         inv_rms[at, :] = jnp.broadcast_to(scale, (ROWS, LANES))
         normed[at, :] = wide * scale
 
-    loads[4].wait()
-    loads[5].wait()
+    for copy in load_gain + load_weight:
+        copy.wait()
     copies[0].wait_recv()
     for tile in range(channels // TILE):
         at = slice(tile * TILE, (tile + 1) * TILE)
@@ -129,14 +140,9 @@
             recv[0], weight[at, :half], (((1,), (1,)), ((), ())), preferred_element_type=jnp.float32
         )
 
+    add_bias(0)
     copies[1].wait_recv()
-    for part in range(HALVES):
-        bias = jnp.sum(recv[part].astype(jnp.float32), axis=0, keepdims=True) / replicas
-        for peer in range(replicas):
-            lane = (peer * bias_share // LANES) * LANES
-            if part * half <= lane < (part + 1) * half:
-                lane -= part * half
-                parts_out[peer, gain_rows : gain_rows + 1, :] = bias[:, lane : lane + LANES]
+    add_bias(1)
 
     inner = jnp.zeros((rows, LANES), jnp.float32)
     part_copies = []
@@ -268,7 +274,7 @@
             pltpu.VMEM((rows, channels), f32),
             pltpu.VMEM((replicas, packed, LANES), f32),
             pltpu.VMEM((replicas, packed, LANES), f32),
-            pltpu.SemaphoreType.DMA((6,)),
+            pltpu.SemaphoreType.DMA((3 + 3 * PIECES,)),
             pltpu.SemaphoreType.DMA((HALVES,)),
             pltpu.SemaphoreType.DMA((HALVES,)),
             pltpu.SemaphoreType.DMA((replicas,)),

time: 16.9 us -> 17 us (level)
  no operation moved by 1% of the time
where the time goes in v3:
time: 17 us; the launch traced here: 16.9 us
  Pallas kernels  15.6 us (92%)
  between operations  1.29 us (8%)
    pallas_call x1, Pallas kernels, per_device(): pl.pallas_call(functools.partial(recover_kernel, sections, replicas), out...  14.6 us
    pallas_call x1, Pallas kernels, per_device(): pl.pallas_call(write_kernel, out_shape=(jax.ShapeDtypeStruct((rows, chann...  1.02 us

profile of v3, /device:TPU:0, one launch (start us, length us, event | category | flops | bytes accessed | tf_op | source)
XLA Modules:
  0.0 16.9 jit_solution(9022526866664778844)
XLA Ops:
  1.3 14.6 %recover.1 = (bf16[128,4096]{1,0:T(8,128)(2,1)S(1)}, f32[8,128]{1,0:T(8,128)S(1)}) custom-call(s32[1]{0:T(128)S(6)} %copy.10.failed, s32[1,2]{1,0:T(1,128)} %unfinished_hbm.1, s32[1,2]{1,0:T(1,128)} %lengths_hbm.1, bf16[1,4096]{1,0:T(2,128)(2,1)} %gain_hbm.1, bf16[128,4096]{1,0:T(8,128)(2,1)} %bitcast.5, bf16[8,64,512]{2,1,0:T(8,128)(2,1)} %bitcast.6, ...), custom_call_target="tpu_custom_call" | custom-call | flops 536870912 | bytes 6291456 | tf_op jit(solution)/shard_map/recover/pallas_call | solution.py:255
  15.8 1.0 %write.1 = (bf16[128,4096]{1,0:T(8,128)(2,1)}, f32[1,512]{1,0:T(1,128)}, f32[1,64]{1,0:T(1,128)}) custom-call(bf16[128,4096]{1,0:T(8,128)(2,1)S(1)} %get-tuple-element.8.dx, f32[8,128]{1,0:T(8,128)S(1)} %get-tuple-element.9.share), custom_call_target="tpu_custom_call" | custom-call | bytes 2097152 | tf_op jit(solution)/shard_map/write/pallas_call | solution.py:306

commit v4 on v3

--- a/solution.py
+++ b/solution.py
@@ -38,6 +38,7 @@
     recv,
     normed,
     inv_rms,
+    totals,
     grad_norm,
     parts_out,
     parts_in,
@@ -124,31 +125,36 @@
 
     for copy in load_acts:
         copy.wait()
-    for block in range(rows // ROWS):
-        at = slice(block * ROWS, (block + 1) * ROWS)
+    def normalize(block, carry):
+        at = pl.ds(pl.multiple_of(block * ROWS, ROWS), ROWS)
         wide = acts[at, :].astype(jnp.float32)
         scale = lax.rsqrt(jnp.mean(wide * wide, axis=1, keepdims=True) + EPSILON)
         inv_rms[at, :] = jnp.broadcast_to(scale, (ROWS, LANES))
         normed[at, :] = wide * scale
-
+        return carry
+
+    lax.fori_loop(0, rows // ROWS, normalize, 0)
     for copy in load_gain + load_weight:
         copy.wait()
     copies[0].wait_recv()
-    for tile in range(channels // TILE):
-        at = slice(tile * TILE, (tile + 1) * TILE)
+
+    def multiply(tile, carry):
+        at = pl.ds(pl.multiple_of(tile * 2 * TILE, 2 * TILE), 2 * TILE)
         grad_norm[:, at] = lax.dot_general(
             recv[0], weight[at, :half], (((1,), (1,)), ((), ())), preferred_element_type=jnp.float32
         )
+        return carry
+
+    lax.fori_loop(0, channels // (2 * TILE), multiply, 0)
 
     add_bias(0)
     copies[1].wait_recv()
     add_bias(1)
 
-    inner = jnp.zeros((rows, LANES), jnp.float32)
-    part_copies = []
     width = min(TILE, gain_chunk)
     first = replica // group
-    for step in range(1, chunks + 1):
+
+    def finish(step, inner):
         chunk = lax.rem(first + step, chunks)
         for piece in range(gain_chunk // width):
             at = pl.ds(pl.multiple_of(chunk * gain_chunk + piece * width, width), width)
@@ -166,29 +172,34 @@
             for row in range(width // LANES):
                 inner = inner + product[:, row * LANES : (row + 1) * LANES]
         for g in range(group):
-            if group == 1 and step == chunks:
-                continue
             peer = chunk * group + g
-            copy = pltpu.make_async_remote_copy(
-                src_ref=parts_out.at[peer],
-                dst_ref=parts_in.at[replica],
-                send_sem=part_send_sem.at[peer],
-                recv_sem=part_recv_sem.at[replica],
-                device_id={"dp": peer},
-                device_id_type=MESH,
-            )
-            if group == 1:
-                copy.start()
-            else:
-                pl.when(peer != replica)(copy.start)
+
+            @pl.when(peer != replica)
+            def _():
+                pltpu.make_async_remote_copy(
+                    src_ref=parts_out.at[peer],
+                    dst_ref=parts_in.at[replica],
+                    send_sem=part_send_sem.at[peer],
+                    recv_sem=part_recv_sem.at[replica],
+                    device_id={"dp": peer},
+                    device_id_type=MESH,
+                ).start()
+
+        return inner
+
+    inner = lax.fori_loop(1, chunks + 1, finish, jnp.zeros((rows, LANES), jnp.float32))
     parts_in[replica] = parts_out[replica]
 
-    inner = jnp.sum(inner, axis=1, keepdims=True) / channels
+    totals[...] = jnp.broadcast_to(jnp.sum(inner, axis=1, keepdims=True) / channels, totals.shape)
     gain = gain_ref[...].astype(jnp.float32)
-    for block in range(rows // ROWS):
-        at = slice(block * ROWS, (block + 1) * ROWS)
-        result = inv_rms[at, :1] * (grad_norm[at, :] * gain - normed[at, :] * inner[at])
+
+    def correct(block, carry):
+        at = pl.ds(pl.multiple_of(block * ROWS, ROWS), ROWS)
+        result = inv_rms[at, :1] * (grad_norm[at, :] * gain - normed[at, :] * totals[at, :1])
         dx_ref[at, :] = result.astype(jnp.bfloat16)
+        return carry
+
+    lax.fori_loop(0, rows // ROWS, correct, 0)
 
     for step in range(1, replicas):
         peer = lax.rem(replica + step, replicas)
@@ -271,6 +282,7 @@
             pltpu.VMEM((HALVES, rows, features // HALVES), bf16),
             pltpu.VMEM((rows, channels), f32),
             pltpu.VMEM((rows, LANES), f32),
+            pltpu.VMEM((rows, LANES), f32),
             pltpu.VMEM((rows, channels), f32),
             pltpu.VMEM((replicas, packed, LANES), f32),
             pltpu.VMEM((replicas, packed, LANES), f32),

time: 17 us -> 17.9 us (1.053)
  Pallas kernels: 15.6 us -> 16.5 us
    pallas_call x1, Pallas kernels: 14.6 us -> 15.5 us  [per_device(): pl.pallas_call(functools.partial(recover_kernel, sections, replicas), out...]
where the time goes in v4:
time: 17.9 us; the launch traced here: 17.8 us
  Pallas kernels  16.5 us (92%)
  between operations  1.29 us (7%)
    pallas_call x1, Pallas kernels, per_device(): pl.pallas_call(functools.partial(recover_kernel, sections, replicas), out...  15.5 us
    pallas_call x1, Pallas kernels, per_device(): pl.pallas_call(write_kernel, out_shape=(jax.ShapeDtypeStruct((rows, chann...  1.02 us

profile of v4, /device:TPU:0, one launch (start us, length us, event | category | flops | bytes accessed | tf_op | source)
XLA Modules:
  0.0 17.8 jit_solution(7436030982504629449)
XLA Ops:
  1.3 15.5 %recover.1 = (bf16[128,4096]{1,0:T(8,128)(2,1)S(1)}, f32[8,128]{1,0:T(8,128)S(1)}) custom-call(s32[1]{0:T(128)S(6)} %copy.10.failed, s32[1,2]{1,0:T(1,128)} %unfinished_hbm.1, s32[1,2]{1,0:T(1,128)} %lengths_hbm.1, bf16[1,4096]{1,0:T(2,128)(2,1)} %gain_hbm.1, bf16[128,4096]{1,0:T(8,128)(2,1)} %bitcast.5, bf16[8,64,512]{2,1,0:T(8,128)(2,1)} %bitcast.6, ...), custom_call_target="tpu_custom_call" | custom-call | flops 536870912 | bytes 6291456 | tf_op jit(solution)/shard_map/recover/pallas_call | solution.py:266
  16.8 1.0 %write.1 = (bf16[128,4096]{1,0:T(8,128)(2,1)}, f32[1,512]{1,0:T(1,128)}, f32[1,64]{1,0:T(1,128)}) custom-call(bf16[128,4096]{1,0:T(8,128)(2,1)S(1)} %get-tuple-element.8.dx, f32[8,128]{1,0:T(8,128)S(1)} %get-tuple-element.9.share), custom_call_target="tpu_custom_call" | custom-call | bytes 2097152 | tf_op jit(solution)/shard_map/write/pallas_call | solution.py:318

commit v5 on v3

--- a/solution.py
+++ b/solution.py
@@ -34,6 +34,7 @@
     acts,
     out_grads,
     weight,
+    turned,
     send,
     recv,
     normed,
@@ -100,17 +101,16 @@
     for copy in load_acts + load_weight + load_gain:
         copy.start()
     is_source = lax.rem(failed[0] + 1, sections) == section
-    for slot in range(slots):
-        picked = out_grads[unfinished[0, slot]].astype(jnp.float32)
-        limit = jnp.where(is_source, lengths[0, slot], 0)
-        position = lax.broadcasted_iota(jnp.int32, picked.shape, 0)
-        picked = jnp.where(position < limit, picked, 0.0).astype(jnp.bfloat16)
-        for part in range(HALVES):
-            send[part, slot * seq : (slot + 1) * seq, :] = picked[:, part * half : (part + 1) * half]
-
-    pl.semaphore_wait(barrier, greeted + replicas - 1)
     copies = []
     for part in range(HALVES):
+        for slot in range(slots):
+            picked = out_grads[unfinished[0, slot], :, part * half : (part + 1) * half].astype(jnp.float32)
+            limit = jnp.where(is_source, lengths[0, slot], 0)
+            position = lax.broadcasted_iota(jnp.int32, picked.shape, 0)
+            picked = jnp.where(position < limit, picked, 0.0).astype(jnp.bfloat16)
+            send[part, slot * seq : (slot + 1) * seq, :] = picked
+        if part == 0:
+            pl.semaphore_wait(barrier, greeted + replicas - 1)
         copy = pltpu.make_async_remote_copy(
             src_ref=send.at[part],
             dst_ref=recv.at[part],
@@ -133,6 +133,9 @@
 
     for copy in load_gain + load_weight:
         copy.wait()
+    for tile in range(channels // TILE):
+        at = slice(tile * TILE, (tile + 1) * TILE)
+        turned[:, at] = weight[at, half:].T
     copies[0].wait_recv()
     for tile in range(channels // TILE):
         at = slice(tile * TILE, (tile + 1) * TILE)
@@ -153,7 +156,7 @@
         for piece in range(gain_chunk // width):
             at = pl.ds(pl.multiple_of(chunk * gain_chunk + piece * width, width), width)
             value = grad_norm[:, at] + lax.dot_general(
-                recv[1], weight[at, half:], (((1,), (1,)), ((), ())), preferred_element_type=jnp.float32
+                recv[1], turned[:, at], (((1,), (0,)), ((), ())), preferred_element_type=jnp.float32
             )
             grad_norm[:, at] = value
             product = value * normed[:, at]
@@ -267,6 +270,7 @@
             pltpu.VMEM((rows, channels), bf16),
             pltpu.VMEM(out_grads.shape[1:], bf16),
             pltpu.VMEM((channels, features), bf16),
+            pltpu.VMEM((features // HALVES, channels), bf16),
             pltpu.VMEM((HALVES, rows, features // HALVES), bf16),
             pltpu.VMEM((HALVES, rows, features // HALVES), bf16),
             pltpu.VMEM((rows, channels), f32),

time: 17 us -> 16.8 us (0.988)
  Pallas kernels: 15.6 us -> 15.4 us
    pallas_call x1, Pallas kernels: 14.6 us -> 14.4 us  [per_device(): pl.pallas_call(functools.partial(recover_kernel, sections, replicas), out...]
where the time goes in v5:
time: 16.8 us; the launch traced here: 16.7 us
  Pallas kernels  15.4 us (92%)
  between operations  1.29 us (8%)
    pallas_call x1, Pallas kernels, per_device(): pl.pallas_call(functools.partial(recover_kernel, sections, replicas), out...  14.4 us
    pallas_call x1, Pallas kernels, per_device(): pl.pallas_call(write_kernel, out_shape=(jax.ShapeDtypeStruct((rows, chann...  1.02 us

profile of v5, /device:TPU:0, one launch (start us, length us, event | category | flops | bytes accessed | tf_op | source)
XLA Modules:
  0.0 16.7 jit_solution(9695203779311320657)
XLA Ops:
  1.3 14.4 %recover.1 = (bf16[128,4096]{1,0:T(8,128)(2,1)S(1)}, f32[8,128]{1,0:T(8,128)S(1)}) custom-call(s32[1]{0:T(128)S(6)} %copy.10.failed, s32[1,2]{1,0:T(1,128)} %unfinished_hbm.1, s32[1,2]{1,0:T(1,128)} %lengths_hbm.1, bf16[1,4096]{1,0:T(2,128)(2,1)} %gain_hbm.1, bf16[128,4096]{1,0:T(8,128)(2,1)} %bitcast.5, bf16[8,64,512]{2,1,0:T(8,128)(2,1)} %bitcast.6, ...), custom_call_target="tpu_custom_call" | custom-call | flops 536870912 | bytes 6291456 | tf_op jit(solution)/shard_map/recover/pallas_call | solution.py:258
  15.7 1.0 %write.1 = (bf16[128,4096]{1,0:T(8,128)(2,1)}, f32[1,512]{1,0:T(1,128)}, f32[1,64]{1,0:T(1,128)}) custom-call(bf16[128,4096]{1,0:T(8,128)(2,1)S(1)} %get-tuple-element.8.dx, f32[8,128]{1,0:T(8,128)S(1)} %get-tuple-element.9.share), custom_call_target="tpu_custom_call" | custom-call | bytes 2097152 | tf_op jit(solution)/shard_map/write/pallas_call | solution.py:310

commit v6 on v5

--- a/solution.py
+++ b/solution.py
@@ -47,6 +47,7 @@
     recv_sem,
     part_send_sem,
     part_recv_sem,
+    round_sem,
 ):
     section = lax.axis_index("section")
     replica = lax.axis_index("dp")
@@ -90,9 +91,27 @@
     if (sections - 2) % sections != 2 % sections:
         greeted = 2
         pl.semaphore_signal(barrier, inc=1, device_id={"section": target}, device_id_type=MESH)
-    for step in range(1, replicas):
-        peer = lax.rem(replica + step, replicas)
-        pl.semaphore_signal(barrier, inc=1, device_id={"dp": peer}, device_id_type=MESH)
+    has_below, has_above = replica >= 2, replica + 2 < replicas
+    mate = replica + 1 - 2 * lax.rem(replica, 2)
+    near = has_below.astype(jnp.int32) + has_above.astype(jnp.int32)
+    rounds = replicas // 2 - 1
+
+    def tell_neighbours(semaphore):
+        @pl.when(has_below)
+        def _():
+            pl.semaphore_signal(semaphore, inc=1, device_id={"dp": replica - 2}, device_id_type=MESH)
+
+        @pl.when(has_above)
+        def _():
+            pl.semaphore_signal(semaphore, inc=1, device_id={"dp": replica + 2}, device_id_type=MESH)
+
+    def wait_round(i):
+        pl.semaphore_wait(round_sem.at[i], near)
+        if i + 1 < rounds:
+            tell_neighbours(round_sem.at[i + 1])
+
+    pl.semaphore_signal(barrier, inc=1, device_id={"dp": mate}, device_id_type=MESH)
+    tell_neighbours(barrier)
 
     for copy in small + load_grads:
         copy.start()
@@ -110,7 +129,7 @@
             picked = jnp.where(position < limit, picked, 0.0).astype(jnp.bfloat16)
             send[part, slot * seq : (slot + 1) * seq, :] = picked
         if part == 0:
-            pl.semaphore_wait(barrier, greeted + replicas - 1)
+            pl.semaphore_wait(barrier, greeted + 1 + near)
         copy = pltpu.make_async_remote_copy(
             src_ref=send.at[part],
             dst_ref=recv.at[part],
@@ -121,6 +140,8 @@
         )
         copy.start()
         copies.append(copy)
+    if rounds > 0:
+        tell_neighbours(round_sem.at[0])
 
     for copy in load_acts:
         copy.wait()
@@ -131,11 +152,15 @@
         inv_rms[at, :] = jnp.broadcast_to(scale, (ROWS, LANES))
         normed[at, :] = wide * scale
 
+    if rounds > 1:
+        wait_round(0)
     for copy in load_gain + load_weight:
         copy.wait()
     for tile in range(channels // TILE):
         at = slice(tile * TILE, (tile + 1) * TILE)
         turned[:, at] = weight[at, half:].T
+    if rounds > 2:
+        wait_round(1)
     copies[0].wait_recv()
     for tile in range(channels // TILE):
         at = slice(tile * TILE, (tile + 1) * TILE)
@@ -146,6 +171,8 @@
     add_bias(0)
     copies[1].wait_recv()
     add_bias(1)
+    for i in range(min(2, max(rounds - 1, 0)), rounds):
+        wait_round(i)
 
     inner = jnp.zeros((rows, LANES), jnp.float32)
     part_copies = []
@@ -283,6 +310,7 @@
             pltpu.SemaphoreType.DMA((HALVES,)),
             pltpu.SemaphoreType.DMA((replicas,)),
             pltpu.SemaphoreType.DMA((replicas,)),
+            pltpu.SemaphoreType.REGULAR((max(replicas // 2 - 1, 1),)),
         ],
         compiler_params=pltpu.CompilerParams(
             collective_id=0, has_side_effects=True, vmem_limit_bytes=28 * 2**20

time: 16.8 us -> 16.3 us (0.970)
  Pallas kernels: 15.4 us -> 14.8 us
    pallas_call x1, Pallas kernels: 14.4 us -> 13.8 us  [per_device(): pl.pallas_call(functools.partial(recover_kernel, sections, replicas), out...]
where the time goes in v6:
time: 16.3 us; the launch traced here: 16.1 us
  Pallas kernels  14.8 us (91%)
  between operations  1.29 us (8%)
    pallas_call x1, Pallas kernels, per_device(): pl.pallas_call(functools.partial(recover_kernel, sections, replicas), out...  13.8 us
    pallas_call x1, Pallas kernels, per_device(): pl.pallas_call(write_kernel, out_shape=(jax.ShapeDtypeStruct((rows, chann...  1.02 us

profile of v6, /device:TPU:0, one launch (start us, length us, event | category | flops | bytes accessed | tf_op | source)
XLA Modules:
  0.0 16.1 jit_solution(17765438687872270559)
XLA Ops:
  1.3 13.8 %recover.1 = (bf16[128,4096]{1,0:T(8,128)(2,1)S(1)}, f32[8,128]{1,0:T(8,128)S(1)}) custom-call(s32[1]{0:T(128)S(6)} %copy.10.failed, s32[1,2]{1,0:T(1,128)} %unfinished_hbm.1, s32[1,2]{1,0:T(1,128)} %lengths_hbm.1, bf16[1,4096]{1,0:T(2,128)(2,1)} %gain_hbm.1, bf16[128,4096]{1,0:T(8,128)(2,1)} %bitcast.5, bf16[8,64,512]{2,1,0:T(8,128)(2,1)} %bitcast.6, ...), custom_call_target="tpu_custom_call" | custom-call | flops 536870912 | bytes 6291456 | tf_op jit(solution)/shard_map/recover/pallas_call | solution.py:285
  15.1 1.0 %write.1 = (bf16[128,4096]{1,0:T(8,128)(2,1)}, f32[1,512]{1,0:T(1,128)}, f32[1,64]{1,0:T(1,128)}) custom-call(bf16[128,4096]{1,0:T(8,128)(2,1)S(1)} %get-tuple-element.8.dx, f32[8,128]{1,0:T(8,128)S(1)} %get-tuple-element.9.share), custom_call_target="tpu_custom_call" | custom-call | bytes 2097152 | tf_op jit(solution)/shard_map/write/pallas_call | solution.py:338
